TPU v7x, 32 devices: a whole 2x2x4 slice. The times are simulated.
32 devices in a mesh: fit: 4 (over x, core), row: 8 (over z, y).
Axes of the slice: x: 2, y: 2, z: 4, core: 2. Of those that a mesh axis runs over, the one named last changes fastest.
Arguments:
- factors: bfloat16 [8192, 12, 512], P('row', 'fit'), may hold values from -2 to 2
Outputs:
- exchange: float32 [4, 8192, 2048], P('fit', 'row')
All inputs are finite; a program needn't handle non-finite values.
Results may differ from a plain program's by a relative error of at most 0.0003.
Values may be sent and summed in bfloat16 or wider, within the bound.
A program may use at most 192 MiB of HBM per device.

v0:
```python
import jax
import jax.numpy as jnp
from jax import lax
from jax.sharding import PartitionSpec as P


def contribution(running, local_part, shard_rows, sub_width):
    groups = running.shape[0]
    product = lax.dot_general(
        local_part, shard_rows, (((1, 2), (1, 2)), ((), ())), preferred_element_type=jnp.float32
    )
    rows_here = product.shape[0]
    placed = jnp.transpose(product.reshape(rows_here, -1, groups, sub_width), (2, 0, 1, 3)).reshape(
        groups, rows_here, -1
    )
    return running + placed


def accumulate(local_rows, remote_rows, initial, sub_width):
    occupied = local_rows.shape[2]
    running = initial
    columns = occupied // 4
    for quarter in range(4):
        local_part = local_rows[:, :, quarter * columns : (quarter + 1) * columns]
        remote_part = remote_rows[:, :, quarter * columns : (quarter + 1) * columns]

        def add_quarter(state, shard_rows, first_row, local_part=local_part):
            return contribution(state, local_part, shard_rows, sub_width)

        running = add_quarter(
            running, lax.all_gather(remote_part, "row", axis=0, tiled=True), jnp.int32(0)
        )
    return running


def per_device(factors):
    row_count = factors.shape[0]
    blocks = lax.axis_size("row")
    groups = lax.axis_size("fit")
    sub_width = row_count // groups
    initial = jnp.zeros((groups, row_count, blocks * sub_width), jnp.float32)
    summed = accumulate(factors, factors, initial, sub_width)
    return lax.psum_scatter(summed, "fit", scatter_dimension=0, tiled=True)


def solution(mesh):
    return jax.shard_map(
        per_device,
        mesh=mesh,
        in_specs=(P("row", "fit", None),),
        out_specs=P("fit", "row", None),
        check_vma=False,
    )
```

profile of v0, /device:TPU:0, one launch (start us, length us, event | category | flops | bytes accessed | tf_op | source)
XLA Modules:
  0.0 798.6 jit_solution(12698665956396815823)
XLA Ops:
  6.5 0.0 copy-start
  6.5 0.0 all-gather.9.cloned.1.call-start
  6.5 3.8 fusion.7
  10.3 0.0 all-gather.9.cloned.1.call-update
  10.3 0.0 all-gather.7.cloned.1.call-start
  10.4 0.7 all-gather.7.cloned.1.call-update
  11.1 0.0 all-gather.5.cloned.1.call-start
  11.1 0.7 all-gather.5.cloned.1.call-update
  11.8 0.0 all-gather.11.cloned.1.call-start
  11.9 0.5 all-gather.11.cloned.1.call-update
  12.4 0.0 reduce-scatter.2.cloned.1.call-start
  12.5 99.8 %all-gather.9.cloned.1.call-done = bf16[8192,3,128]{2,0,1:T(8,128)(2,1)} async-done(((bf16[1024,3,128]{2,0,1:T(8,128)(2,1)}), bf16[8192,3,128]{2,0,1:T(8,128)(2,1)}) %all-gather.9.cloned.1.call-update) | async-done | bytes 6291472 | tf_op jit(solution)/shard_map/all_gather | solution.py:31
  112.2 0.0 copy-done
  112.2 17.6 %fusion.1 = f32[1024,8192,1]{1,0,2:T(8,128)} fusion(bf16[8192,3,128]{2,0,1:T(8,128)(2,1)} %all-gather.9.cloned.1.call-done, bf16[1024,3,512]{2,0,1:T(8,128)(2,1)S(1)} %copy-done), kind=kOutput, calls=%fused_computation.4 | convolution fusion | flops 6442450944 | bytes 40632320 | tf_op jit(solution)/shard_map/dot_general | solution.py:9
  129.8 81.8 %all-gather.7.cloned.1.call-done = bf16[8192,3,128]{2,0,1:T(8,128)(2,1)} async-done(((bf16[1024,3,128]{2,0,1:T(8,128)(2,1)}), bf16[8192,3,128]{2,0,1:T(8,128)(2,1)}) %all-gather.7.cloned.1.call-update) | async-done | bytes 6291472 | tf_op jit(solution)/shard_map/all_gather | solution.py:31
  211.7 17.6 %fusion.3 = f32[1024,8192,1]{1,0,2:T(8,128)} fusion(bf16[8192,3,128]{2,0,1:T(8,128)(2,1)} %all-gather.7.cloned.1.call-done, bf16[1024,3,512]{2,0,1:T(8,128)(2,1)S(1)} %copy-done), kind=kOutput, calls=%fused_computation.6 | convolution fusion | flops 6442450944 | bytes 40632320 | tf_op jit(solution)/shard_map/dot_general | solution.py:9
  229.2 81.9 %all-gather.5.cloned.1.call-done = bf16[8192,3,128]{2,0,1:T(8,128)(2,1)} async-done(((bf16[1024,3,128]{2,0,1:T(8,128)(2,1)}), bf16[8192,3,128]{2,0,1:T(8,128)(2,1)}) %all-gather.5.cloned.1.call-update) | async-done | bytes 6291472 | tf_op jit(solution)/shard_map/all_gather | solution.py:31
  311.1 17.7 %fusion.5 = f32[1024,8192,1]{1,0,2:T(8,128)} fusion(bf16[8192,3,128]{2,0,1:T(8,128)(2,1)} %all-gather.5.cloned.1.call-done, bf16[1024,3,512]{2,0,1:T(8,128)(2,1)S(1)} %copy-done), kind=kOutput, calls=%fused_computation.8 | convolution fusion | flops 6442450944 | bytes 40632320 | tf_op jit(solution)/shard_map/dot_general | solution.py:9
  328.8 81.6 %all-gather.11.cloned.1.call-done = bf16[8192,3,128]{2,0,1:T(8,128)(2,1)} async-done(((bf16[1024,3,128]{2,0,1:T(8,128)(2,1)}), bf16[8192,3,128]{2,0,1:T(8,128)(2,1)}) %all-gather.11.cloned.1.call-update) | async-done | bytes 6291472 | tf_op jit(solution)/shard_map/all_gather | solution.py:31
  410.4 45.8 %bitcast_add_fusion = f32[1024,8192]{1,0:T(8,128)} fusion(f32[1024,8192,1]{1,0,2:T(8,128)} %fusion.1, f32[1024,8192,1]{1,0,2:T(8,128)} %fusion.3, f32[1024,8192,1]{1,0,2:T(8,128)} %fusion.5, bf16[8192,3,128]{2,0,1:T(8,128)(2,1)} %all-gather.11.cloned.1.call-done, bf16[1024,3,512]{2,0,1:T(8,128)(2,1)S(1)} %copy-done), kind=kOutput, calls=%fused_computation | convolution fusion | flops 6467616768 | bytes 141295616 | tf_op jit(solution)/shard_map/dot_general | solution.py:9
  456.1 39.6 %reshape.16 = f32[1024,8,4,256]{3,2,1,0:T(4,128)} reshape(f32[1024,8192]{1,0:T(8,128)} %bitcast_add_fusion) | data formatting | bytes 67108864 | tf_op jit(solution)/shard_map/add | solution.py:16
  495.7 27.6 %copy.2 = f32[4,1024,8,256]{3,2,1,0:T(8,128)} copy(f32[4,1024,8,256]{3,0,2,1:T(4,128)} %bitcast.24) | data formatting | bytes 67108864 | tf_op jit(solution)/shard_map/add | solution.py:16
  523.3 35.5 %add.30 = f32[4,1024,2048]{2,1,0:T(8,128)} reshape(f32[4,1024,8,256]{3,2,1,0:T(8,128)} %copy.2) | data formatting | bytes 67108864 | tf_op jit(solution)/shard_map/add | solution.py:16
  558.8 0.0 reduce-scatter.2.cloned.1.call-update
  558.8 233.3 %reduce-scatter.2.cloned.1.call-done = f32[1,1024,2048]{2,1,0:T(8,128)} async-done(((f32[4,1024,2048]{2,1,0:T(8,128)}), f32[1,1024,2048]{2,1,0:T(8,128)}) %reduce-scatter.2.cloned.1.call-update) | async-done | bytes 8388624 | tf_op jit(solution)/shard_map/reduce_scatter | solution.py:43
Async XLA Ops:
  6.5 105.7 %copy-start = (bf16[1024,3,512]{2,0,1:T(8,128)(2,1)S(1)}, bf16[1024,3,512]{2,0,1:T(8,128)(2,1)}, u32[]{:S(2)}) copy-start(bf16[1024,3,512]{2,0,1:T(8,128)(2,1)} %param.1) | copy-start | bytes 9437188
  6.5 105.7 %all-gather.9.cloned.1.call-start = ((), (), s32[]{:S(2)}) async-start(), calls=%async_computation.3 | async-start | bytes 7077888 | tf_op jit(solution)/shard_map/all_gather | solution.py:31
  10.3 201.3 %all-gather.7.cloned.1.call-start = ((), (), s32[]{:S(2)}) async-start(), calls=%async_computation.2 | async-start | bytes 7077888 | tf_op jit(solution)/shard_map/all_gather | solution.py:31
  11.1 300.0 %all-gather.5.cloned.1.call-start = ((), (), s32[]{:S(2)}) async-start(), calls=%async_computation.1 | async-start | bytes 7077888 | tf_op jit(solution)/shard_map/all_gather | solution.py:31
  11.8 398.6 %all-gather.11.cloned.1.call-start = ((), (), s32[]{:S(2)}) async-start(), calls=%async_computation.4 | async-start | bytes 7077888 | tf_op jit(solution)/shard_map/all_gather | solution.py:31
  12.4 779.7 %reduce-scatter.2.cloned.1.call-start = ((), (), s32[]{:S(2)}) async-start(), calls=%async_computation.5 | async-start | bytes 41943040 | tf_op jit(solution)/shard_map/reduce_scatter | solution.py:43
Sparse Core Ops, SparseCore 0:
  10.5 101.7 all-gather.8
  114.4 97.2 all-gather.6
  213.8 97.2 all-gather.4
  313.1 97.1 all-gather.10
  558.9 233.1 reduce-scatter.1
where the time goes:
time: 801 us; the launch traced here: 799 us
  waiting for transfers between devices  580 us (72%)
  local copies, waits for them, and re-layouts  106 us (13%)
  matrix products  98.6 us (12%)
  between operations  13.1 us (2%)
    all_gather x4, waiting for transfers between devices, accumulate(): lax.all_gather(remote_part, 'row', axis=0, tiled=True)  345 us
    reduce_scatter x1, waiting for transfers between devices, per_device(): return lax.psum_scatter(summed, 'fit', scatter_dimension=0, tiled=True)  233 us
    add x3, local copies, waits for them, and re-layouts, contribution(): return running + placed  103 us
    dot_general x4, matrix products, contribution(): lax.dot_general(local_part, shard_rows, (((1, 2), (1, 2)), ((), ())), pre...  98.6 us
  transfers between devices with their start and end apart: 5, of which 5 were waited for; matrix products, arithmetic and copies ran while one was open for 7% of the time, Pallas kernels for 0%

commit v1 on v0

v1 whole, which is shorter than its diff:
```python
import jax
import jax.numpy as jnp
from jax import lax
from jax.sharding import PartitionSpec as P


def per_device(factors):
    row_count, local_funcs, occupied = factors.shape
    groups = lax.axis_size("fit")
    blocks = lax.axis_size("row")
    sub_width = row_count // groups
    pieces = factors.reshape(groups, sub_width, local_funcs * occupied)
    mine = lax.all_to_all(pieces, "fit", split_axis=0, concat_axis=0)
    columns = lax.all_gather(mine, "row", axis=0)
    rows = lax.all_gather(factors.reshape(row_count, local_funcs * occupied), "fit", axis=0)
    out = lax.dot_general(
        rows, columns, (((0, 2), (1, 3)), ((), ())), preferred_element_type=jnp.float32
    )
    return out.reshape(1, row_count, blocks * sub_width)


def solution(mesh):
    return jax.shard_map(
        per_device,
        mesh=mesh,
        in_specs=(P("row", "fit", None),),
        out_specs=P("fit", "row", None),
        check_vma=False,
    )
```

time: 801 us -> 662 us (0.83)
  local copies, waits for them, and re-layouts: 106 us -> 24.2 us
  blocking collectives: 0 us -> 72.9 us
  matrix products: 98.6 us -> 34.4 us
  waiting for transfers between devices: 580 us -> 517 us
    reduce_scatter x1 -> x0, waiting for transfers between devices: 233 us -> none  [per_device(): return lax.psum_scatter(summed, 'fit', scatter_dimension=0, tiled=True)]
    all_gather x4 -> x2, waiting for transfers between devices: 345 us -> 517 us  [the longest x1 482 us: per_device(): columns = lax.all_gather(mine, 'row', axis=0)]
    add x3 -> x0, local copies, waits for them, and re-layouts: 103 us -> none  [contribution(): return running + placed]
    all_to_all x0 -> x1, blocking collectives: none -> 72.9 us  [per_device(): mine = lax.all_to_all(pieces, 'fit', split_axis=0, concat_axis=0)]
    dot_general x4 -> x1, matrix products: 98.6 us -> 34.4 us  [per_device(): lax.dot_general(rows, columns, (((0, 2), (1, 3)), ((), ())), preferred_el...]
    reshape x0 -> x3, local copies, waits for them, and re-layouts: none -> 15.3 us  [the longest x1 9.12 us: per_device(): return out.reshape(1, row_count, blocks * sub_width)]
  transfers between devices with their start and end apart: 5 -> 2, of which waited for: 5 -> 2; matrix products, arithmetic and copies ran while one was open for 7% -> 1% of each run, Pallas kernels for 0% -> 0%
where the time goes in v1:
time: 662 us
  waiting for transfers between devices  517 us (78%)
  blocking collectives  72.9 us (11%)
  matrix products  34.4 us (5%)
  local copies, waits for them, and re-layouts  24.2 us (4%)
  between operations  13.4 us (2%)
    all_gather x1, waiting for transfers between devices, per_device(): columns = lax.all_gather(mine, 'row', axis=0)  482 us
    all_to_all x1, blocking collectives, per_device(): mine = lax.all_to_all(pieces, 'fit', split_axis=0, concat_axis=0)  72.9 us
    all_gather x1, waiting for transfers between devices, per_device(): lax.all_gather(factors.reshape(row_count, local_funcs * occupied), 'fit',...  34.6 us
    dot_general x1, matrix products, per_device(): lax.dot_general(rows, columns, (((0, 2), (1, 3)), ((), ())), preferred_el...  34.4 us
  transfers between devices with their start and end apart: 2, of which 2 were waited for; matrix products, arithmetic and copies ran while one was open for 1% of the time, Pallas kernels for 0%

profile of v1, /device:TPU:0, one launch (start us, length us, event | category | flops | bytes accessed | tf_op | source)
XLA Modules:
  0.0 662.0 jit_solution(14570974016559412265)
XLA Ops:
  6.5 0.0 all-gather.4.cloned.1.call-start
  6.5 3.2 copy.9
  9.7 2.9 copy.10
  12.7 0.0 all-gather.4.cloned.1.call-update
  12.7 0.0 all-gather.6.cloned.1.call-start
  12.7 3.9 reshape.6
  16.7 2.3 copy.12
  19.0 72.9 %all_to_all.5 = bf16[4,256,1536]{1,2,0:T(8,128)(2,1)S(1)} all-to-all(bf16[4,256,1536]{1,2,0:T(8,128)(2,1)S(1)} %copy.12), channel_id=1, replica_groups=mesh['fit'=4,'row'=8] {'fit'}, dimensions={0} | all-to-all | bytes 6291456 | tf_op jit(solution)/shard_map/all_to_all | solution.py:13
  91.9 2.8 copy.13
  94.7 0.0 all-gather.6.cloned.1.call-update
  94.7 34.6 %all-gather.4.cloned.1.call-done = bf16[4,1024,1536]{2,1,0:T(8,128)(2,1)} async-done(((bf16[1,1024,1536]{2,1,0:T(8,128)(2,1)}), bf16[4,1024,1536]{2,1,0:T(8,128)(2,1)}) %all-gather.4.cloned.1.call-update) | async-done | bytes 12582928 | tf_op jit(solution)/shard_map/all_gather | solution.py:15
  129.3 482.3 %all-gather.6.cloned.1.call-done = bf16[32,256,1536]{2,1,0:T(8,128)(2,1)} async-done(((bf16[4,256,1536]{2,1,0:T(8,128)(2,1)}), bf16[32,256,1536]{2,1,0:T(8,128)(2,1)}) %all-gather.6.cloned.1.call-update) | async-done | bytes 25165840 | tf_op jit(solution)/shard_map/all_gather | solution.py:14
  611.6 34.4 %fusion = f32[1024,8,256,1]{0,2,3,1:T(8,128)} fusion(bf16[8,4,256,1536]{3,2,1,0:T(8,128)(2,1)} %bitcast.14, bf16[4,1024,1536]{2,1,0:T(8,128)(2,1)} %all-gather.4.cloned.1.call-done), kind=kOutput, calls=%fused_computation | convolution fusion | flops 25769803776 | bytes 46137344 | tf_op jit(solution)/shard_map/dot_general | solution.py:16
  646.0 9.1 %copy.14 = f32[1,1024,2048]{2,1,0:T(8,128)} copy(f32[1,1024,2048]{1,2,0:T(8,128)} %bitcast.13) | data formatting | bytes 16777216 | tf_op jit(solution)/shard_map/reshape | solution.py:19
Async XLA Ops:
  6.5 122.7 %all-gather.4.cloned.1.call-start = ((), (), s32[]{:S(2)}) async-start(), calls=%async_computation.1 | async-start | bytes 15728640 | tf_op jit(solution)/shard_map/all_gather | solution.py:15
  12.7 598.9 %all-gather.6.cloned.1.call-start = ((), (), s32[]{:S(2)}) async-start(), calls=%async_computation.2 | async-start | bytes 28311552 | tf_op jit(solution)/shard_map/all_gather | solution.py:14
Sparse Core Ops, SparseCore 0:
  12.8 116.4 all-gather.3
  130.8 480.7 all-gather.5

commit v2 on v1

--- a/solution.py
+++ b/solution.py
@@ -1,10 +1,18 @@
+import functools
+
 import jax
 import jax.numpy as jnp
 from jax import lax
+from jax.experimental import pallas as pl
+from jax.experimental.pallas import tpu as pltpu
 from jax.sharding import PartitionSpec as P
 
-
-def per_device(factors):
+MESH = pl.DeviceIdType.MESH
+Z_SIZE = 4
+Y_SIZE = 2
+
+
+def gathered_by_collectives(factors):
     row_count, local_funcs, occupied = factors.shape
     groups = lax.axis_size("fit")
     blocks = lax.axis_size("row")
@@ -19,6 +27,239 @@
     return out.reshape(1, row_count, blocks * sub_width)
 
 
+def kernel(first, a_ref, out_ref, rows, cols, fit_send, fit_recv, send_sem, recv_sem):
+    f = lax.axis_index("fit")
+    r = lax.axis_index("row")
+    z = r // Y_SIZE
+    y = r % Y_SIZE
+    core_mate = f + 1 - 2 * (f % 2)
+    x_peer = (f + 2) % 4
+    diagonal = (core_mate + 2) % 4
+    subs = (f, core_mate, x_peer, diagonal)
+    row_count, width = a_ref.shape
+    sub = row_count // 4
+    has_up = z < Z_SIZE - 1
+    has_down = z > 0
+    y_mate = z * Y_SIZE + 1 - y
+    parts = [(0, 0, first), (0, first, width - first)] + [(q, 0, width) for q in (1, 2, 3)]
+
+    def row_slice(s):
+        return pl.ds(pl.multiple_of(s * sub, sub), sub)
+
+    def greet(fit, row):
+        pl.semaphore_signal(
+            pltpu.get_barrier_semaphore(), inc=1, device_id=(fit, row), device_id_type=MESH
+        )
+
+    greet(core_mate, r)
+    greet(x_peer, r)
+    greet(f, y_mate)
+    pl.when(has_up)(lambda: greet(f, r + Y_SIZE))
+    pl.when(has_down)(lambda: greet(f, r - Y_SIZE))
+    pl.semaphore_wait(
+        pltpu.get_barrier_semaphore(), 3 + has_up.astype(jnp.int32) + has_down.astype(jnp.int32)
+    )
+
+    def fit_copy(q, j):
+        if q == 2:
+            target, s = x_peer, subs[2 ^ j]
+        else:
+            target, s = core_mate, subs[1 ^ j]
+        source = rows.at[1, row_slice(s)] if q == 3 else a_ref.at[row_slice(s)]
+        return pltpu.make_async_remote_copy(
+            src_ref=source,
+            dst_ref=rows.at[q - 1, row_slice(s)],
+            send_sem=fit_send.at[q - 1, j],
+            recv_sem=fit_recv.at[q - 1, j],
+            device_id=(target, r),
+            device_id_type=MESH,
+        )
+
+    def fit_wait(q, j):
+        landed = rows.at[q - 1, row_slice(subs[j])]
+        pltpu.make_async_remote_copy(
+            src_ref=landed,
+            dst_ref=landed,
+            send_sem=fit_send.at[q - 1, j],
+            recv_sem=fit_recv.at[q - 1, j],
+            device_id=(core_mate, r),
+            device_id_type=MESH,
+        ).wait_recv()
+
+    def slot_of(block, part):
+        q, begin, size = parts[part]
+        return cols.at[block, q, :, pl.ds(begin, size)]
+
+    def own_source(part):
+        q, begin, size = parts[part]
+        if q == 0:
+            return a_ref.at[row_slice(f), pl.ds(begin, size)]
+        return rows.at[q - 1, row_slice(f), pl.ds(begin, size)]
+
+    def plane_copy(direction, block, part, source=None):
+        target = (r + Y_SIZE, r - Y_SIZE, y_mate)[direction]
+        slot = slot_of(block, part)
+        return pltpu.make_async_remote_copy(
+            src_ref=slot if source is None else source,
+            dst_ref=slot,
+            send_sem=send_sem.at[direction, block, part],
+            recv_sem=recv_sem.at[block, part],
+            device_id=(f, target),
+            device_id_type=MESH,
+        )
+
+    def plane_wait(block, part):
+        plane_copy(2, block, part).wait_recv()
+
+    def send_own(part):
+        source = own_source(part)
+        pl.when(has_up)(lambda: plane_copy(0, r, part, source).start())
+        pl.when(has_down)(lambda: plane_copy(1, r, part, source).start())
+        plane_copy(2, r, part, source).start()
+
+    fit_copy(2, 0).start()
+    fit_copy(1, 0).start()
+    send_own(0)
+    send_own(1)
+    fit_copy(2, 1).start()
+    for j in (1, 2, 3):
+        fit_copy(1, j).start()
+    fit_wait(1, 0)
+    send_own(2)
+    plane_wait(y_mate, 0)
+    pl.when(has_up)(lambda: plane_copy(0, y_mate, 0).start())
+    pl.when(has_down)(lambda: plane_copy(1, y_mate, 0).start())
+    fit_wait(2, 0)
+    send_own(3)
+    fit_copy(2, 2).start()
+    fit_wait(2, 1)
+    fit_copy(3, 0).start()
+    fit_copy(2, 3).start()
+    fit_copy(3, 1).start()
+    fit_wait(3, 0)
+    send_own(4)
+
+    dims = (((1,), (1,)), ((), ()))
+
+    def multiply(operand, block):
+        tile = min(512, row_count)
+
+        @pl.loop(0, row_count // tile)
+        def _(i):
+            here = pl.ds(pl.multiple_of(i * tile, tile), tile)
+            total = lax.dot_general(
+                a_ref[here, :], operand(0), dims, preferred_element_type=jnp.float32
+            )
+            for q in (1, 2, 3):
+                total += lax.dot_general(
+                    rows[q - 1, here, :], operand(q), dims, preferred_element_type=jnp.float32
+                )
+            out_ref[here, pl.ds(pl.multiple_of(block * sub, sub), sub)] = total
+
+    def finish_fit():
+        for j in (2, 3):
+            fit_wait(2, j)
+            fit_copy(3, j ^ 1).start()
+        for j in (1, 2, 3):
+            fit_wait(1, j)
+            fit_wait(3, j)
+        multiply(
+            lambda q: a_ref[row_slice(f), :] if q == 0 else rows[q - 1, row_slice(f), :], r
+        )
+
+    def stage(d, carry):
+        for part, mate in [(0, 0), (0, 1), (1, 0), (2, 0), (3, 0), (4, 0)]:
+            line = y if mate == 0 else 1 - y
+            for side in (0, 1):
+                far = z - d if side == 0 else z + d
+                block = far * Y_SIZE + line
+
+                @pl.when((far >= 0) if side == 0 else (far < Z_SIZE))
+                def _(block=block, part=part, side=side):
+                    plane_wait(block, part)
+                    onward = has_up if side == 0 else has_down
+                    pl.when(onward)(lambda: plane_copy(side, block, part).start())
+                    if part > 0:
+                        plane_copy(2, block, part).start()
+
+        pl.when(d == 1)(finish_fit)
+
+        def one_block(t, carry):
+            side = t % 2
+            mate = t // 2
+            away = d - mate
+            far = z + (2 * side - 1) * away
+            block = far * Y_SIZE + y + mate * (1 - 2 * y)
+
+            @pl.when((far >= 0) & (far < Z_SIZE) & ((away > 0) | (side == 0)))
+            def _():
+                @pl.when(mate == 1)
+                def _():
+                    for part in (1, 2, 3, 4):
+                        plane_wait(block, part)
+
+                multiply(lambda q: cols[block, q], block)
+
+            return carry
+
+        return lax.fori_loop(0, 4, one_block, carry)
+
+    lax.fori_loop(1, Z_SIZE + 1, stage, 0)
+
+    for q in (1, 2, 3):
+        for j in range(4):
+            fit_copy(q, j).wait_send()
+
+    def drain(far, carry):
+        for part in range(5):
+            for mate in (0, 1):
+                if mate == 1 and part > 0:
+                    continue
+                block = far * Y_SIZE + (y if mate == 0 else 1 - y)
+                pl.when(has_up & (far <= z))(lambda: plane_copy(0, block, part).wait_send())
+                pl.when(has_down & (far >= z))(lambda: plane_copy(1, block, part).wait_send())
+                if part > 0:
+                    plane_copy(2, block, part).wait_send()
+        return carry
+
+    lax.fori_loop(0, Z_SIZE, drain, 0)
+    plane_copy(2, r, 0).wait_send()
+
+
+def per_device(factors):
+    row_count, local_funcs, occupied = factors.shape
+    groups = lax.axis_size("fit")
+    blocks = lax.axis_size("row")
+    if (groups, blocks) != (4, Y_SIZE * Z_SIZE):
+        return gathered_by_collectives(factors)
+    sub = row_count // groups
+    width = local_funcs * occupied
+    out_shape = jax.ShapeDtypeStruct((row_count, blocks * sub), jnp.float32)
+    out = pl.pallas_call(
+        functools.partial(kernel, (local_funcs - 1) * occupied),
+        out_shape=out_shape,
+        in_specs=[pl.BlockSpec(memory_space=pltpu.VMEM)],
+        out_specs=pl.BlockSpec(memory_space=pltpu.VMEM),
+        scratch_shapes=[
+            pltpu.VMEM((groups - 1, row_count, width), factors.dtype),
+            pltpu.VMEM((blocks, groups, sub, width), factors.dtype),
+            pltpu.SemaphoreType.DMA((3, 4)),
+            pltpu.SemaphoreType.DMA((3, 4)),
+            pltpu.SemaphoreType.DMA((3, blocks, 5)),
+            pltpu.SemaphoreType.DMA((blocks, 5)),
+        ],
+        compiler_params=pltpu.CompilerParams(
+            collective_id=0, has_side_effects=True, vmem_limit_bytes=58 * 2**20
+        ),
+        cost_estimate=pl.CostEstimate(
+            flops=2 * row_count * blocks * sub * groups * width,
+            bytes_accessed=4 * row_count * blocks * sub,
+            transcendentals=0,
+        ),
+    )(factors.reshape(row_count, width))
+    return out.reshape(1, row_count, blocks * sub)
+
+
 def solution(mesh):
     return jax.shard_map(
         per_device,

time: 662 us -> 284 us (0.43)
  waiting for transfers between devices: 517 us -> 0 us
  Pallas kernels: 0 us -> 270 us
  blocking collectives: 72.9 us -> 0 us
  matrix products: 34.4 us -> 0 us
  between operations: 13.4 us -> 0.02 us
  local copies, waits for them, and re-layouts: 24.2 us -> 14 us
    all_gather x2 -> x0, waiting for transfers between devices: 517 us -> none  [the longest x1 482 us: per_device(): columns = lax.all_gather(mine, 'row', axis=0)]
    pallas_call x0 -> x1, Pallas kernels: none -> 270 us  [per_device(): pl.pallas_call(functools.partial(kernel, (local_funcs - 1) * occupied), o...]
    all_to_all x1 -> x0, blocking collectives: 72.9 us -> none  [per_device(): mine = lax.all_to_all(pieces, 'fit', split_axis=0, concat_axis=0)]
    dot_general x1 -> x0, matrix products: 34.4 us -> none  [per_device(): lax.dot_general(rows, columns, (((0, 2), (1, 3)), ((), ())), preferred_el...]
    reshape x3 -> x1, local copies, waits for them, and re-layouts: 15.3 us -> 2.93 us  [per_device(): factors.reshape(row_count, width)]
    unnamed x1 -> x2, local copies, waits for them, and re-layouts: 3.18 us -> 11.1 us
  transfers between devices with their start and end apart: 2 -> 0, of which waited for: 2 -> 0; matrix products, arithmetic and copies ran while one was open for 1% -> 0% of each run, Pallas kernels for 0% -> 0%
where the time goes in v2:
time: 284 us
  Pallas kernels  270 us (95%)
  local copies, waits for them, and re-layouts  14 us (5%)
    pallas_call x1, Pallas kernels, per_device(): pl.pallas_call(functools.partial(kernel, (local_funcs - 1) * occupied), o...  270 us
    unnamed x2, local copies, waits for them, and re-layouts  11.1 us

profile of v2, /device:TPU:0, one launch (start us, length us, event | category | flops | bytes accessed | tf_op | source)
XLA Modules:
  0.0 283.7 jit_solution(2009174473843875258)
XLA Ops:
  0.0 3.2 %copy.3 = bf16[1024,3,512]{0,2,1:T(8,128)(2,1)S(1)} copy(bf16[1024,3,512]{2,0,1:T(8,128)(2,1)} %param.1) | data formatting | bytes 6291456 | tf_op args[0]
  3.2 2.9 %copy.4.a_ref = bf16[1024,1536]{1,0:T(8,128)(2,1)} copy(bf16[1024,1536]{0,1:T(8,128)(2,1)S(1)} %bitcast.2) | data formatting | bytes 6291456 | tf_op jit(solution)/shard_map/reshape | solution.py:259
  6.1 269.7 %shard_map.17 = f32[1024,2048]{1,0:T(8,128)} custom-call(bf16[1024,1536]{1,0:T(8,128)(2,1)} %copy.4.a_ref), custom_call_target="tpu_custom_call" | custom-call | flops 25769803776 | bytes 8388608 | tf_op jit(solution)/shard_map/pallas_call | solution.py:238
  275.8 7.9 %copy.6 = f32[1,1024,2048]{2,1,0:T(8,128)} copy(f32[1,1024,2048]{2,1,0:T(8,128)} %bitcast.3) | data formatting | bytes 16777216

commit v3 on v1

--- a/solution.py
+++ b/solution.py
@@ -1,10 +1,16 @@
 import jax
 import jax.numpy as jnp
 from jax import lax
+from jax.experimental import pallas as pl
+from jax.experimental.pallas import tpu as pltpu
 from jax.sharding import PartitionSpec as P
 
-
-def per_device(factors):
+MESH = pl.DeviceIdType.MESH
+Z_SIZE = 4
+Y_SIZE = 2
+
+
+def gathered_by_collectives(factors):
     row_count, local_funcs, occupied = factors.shape
     groups = lax.axis_size("fit")
     blocks = lax.axis_size("row")
@@ -19,6 +25,342 @@
     return out.reshape(1, row_count, blocks * sub_width)
 
 
+def kernel(a_ref, out_ref, acc, rows, near, cols, tiles, fit_send, fit_recv, near_send, near_recv,
+           send_sem, recv_sem, tile_send, tile_recv, out_sem):
+    f = lax.axis_index("fit")
+    r = lax.axis_index("row")
+    z = r // Y_SIZE
+    y = r % Y_SIZE
+    core_mate = f + 1 - 2 * (f % 2)
+    x_peer = (f + 2) % 4
+    diagonal = (core_mate + 2) % 4
+    subs = (f, core_mate, x_peer, diagonal)
+    row_count, width = a_ref.shape
+    sub = row_count // 4
+    half = z // 2
+    end_z, inner_z = 3 * half, 1 + half
+    far_inner_z, far_end_z = 2 - half, 3 - 3 * half
+    is_end = z == end_z
+    is_inner = z == inner_z
+
+    def node(at_z, line):
+        return at_z * Y_SIZE + line
+
+    end0, end1 = node(end_z, y), node(end_z, 1 - y)
+    inner0, inner1 = node(inner_z, y), node(inner_z, 1 - y)
+    far_inner0, far_inner1 = node(far_inner_z, y), node(far_inner_z, 1 - y)
+    far_end0, far_end1 = node(far_end_z, y), node(far_end_z, 1 - y)
+    y_mate = node(z, 1 - y)
+    partner = node(end_z + inner_z - z, y)
+    PARTNER, FAR, MATE = 0, 1, 2
+    targets = (partner, far_inner0, y_mate)
+    quarters = range(4)
+
+    def row_slice(s):
+        return pl.ds(pl.multiple_of(s * sub, sub), sub)
+
+    def col_slice(block):
+        return pl.ds(pl.multiple_of(block * sub, sub), sub)
+
+    def greet(fit, row):
+        pl.semaphore_signal(
+            pltpu.get_barrier_semaphore(), inc=1, device_id=(fit, row), device_id_type=MESH
+        )
+
+    greet(core_mate, r)
+    greet(x_peer, r)
+    greet(f, y_mate)
+    greet(f, partner)
+    pl.when(is_inner)(lambda: greet(f, far_inner0))
+    pl.semaphore_wait(pltpu.get_barrier_semaphore(), 4 + is_inner.astype(jnp.int32))
+
+    def fit_copy(q, j):
+        if q == 2:
+            target, s = x_peer, subs[2 ^ j]
+        else:
+            target, s = core_mate, subs[1 ^ j]
+        source = rows.at[1, row_slice(s)] if q == 3 else a_ref.at[row_slice(s)]
+        return pltpu.make_async_remote_copy(
+            src_ref=source,
+            dst_ref=rows.at[q - 1, row_slice(s)],
+            send_sem=fit_send.at[q - 1, j],
+            recv_sem=fit_recv.at[q - 1, j],
+            device_id=(target, r),
+            device_id_type=MESH,
+        )
+
+    def fit_wait(q, j):
+        landed = rows.at[q - 1, row_slice(subs[j])]
+        pltpu.make_async_remote_copy(
+            src_ref=landed,
+            dst_ref=landed,
+            send_sem=fit_send.at[q - 1, j],
+            recv_sem=fit_recv.at[q - 1, j],
+            device_id=(core_mate, r),
+            device_id_type=MESH,
+        ).wait_recv()
+
+    def near_copy(j, q):
+        if j == 3:
+            source, target = near.at[1, q ^ 1], core_mate
+        else:
+            source, target = cols.at[end0, q ^ j], (core_mate if j == 1 else x_peer)
+        return pltpu.make_async_remote_copy(
+            src_ref=source,
+            dst_ref=near.at[j - 1, q],
+            send_sem=near_send.at[j - 1, q],
+            recv_sem=near_recv.at[j - 1, q],
+            device_id=(target, r),
+            device_id_type=MESH,
+        )
+
+    def plane_copy(direction, block, q, source=None):
+        slot = cols.at[block, q]
+        return pltpu.make_async_remote_copy(
+            src_ref=slot if source is None else source,
+            dst_ref=slot,
+            send_sem=send_sem.at[direction, block, q],
+            recv_sem=recv_sem.at[block, q],
+            device_id=(f, targets[direction]),
+            device_id_type=MESH,
+        )
+
+    def plane_wait(block, q):
+        plane_copy(MATE, block, q).wait_recv()
+
+    def pass_on(block, q, *directions):
+        plane_wait(block, q)
+        for direction in directions:
+            plane_copy(direction, block, q).start()
+
+    def send_own(q):
+        source = (a_ref if q == 0 else rows.at[q - 1]).at[row_slice(f)]
+        pl.when(is_inner)(lambda: plane_copy(FAR, r, q, source).start())
+        plane_copy(PARTNER, r, q, source).start()
+        plane_copy(MATE, r, q, source).start()
+
+    def tile_copy(block, k, j):
+        return pltpu.make_async_remote_copy(
+            src_ref=tiles.at[k, j],
+            dst_ref=acc.at[row_slice(subs[j]), col_slice(block)],
+            send_sem=tile_send.at[k, j],
+            recv_sem=tile_recv.at[k, j],
+            device_id=(f, partner),
+            device_id_type=MESH,
+        )
+
+    def out_copy(block):
+        return pltpu.make_async_copy(
+            acc.at[:, col_slice(block)], out_ref.at[:, col_slice(block)], out_sem.at[block]
+        )
+
+    dims = (((1,), (1,)), ((), ()))
+
+    def dot(left, right):
+        return lax.dot_general(left, right, dims, preferred_element_type=jnp.float32)
+
+    def multiply(operand, block):
+        tile = min(512, row_count)
+
+        @pl.loop(0, row_count // tile)
+        def _(i):
+            here = pl.ds(pl.multiple_of(i * tile, tile), tile)
+            total = dot(a_ref[here, :], operand(0))
+            for q in (1, 2, 3):
+                total += dot(rows[q - 1, here, :], operand(q))
+            acc[here, col_slice(block)] = total
+
+        out_copy(block).start()
+
+    def multiply_block(block):
+        multiply(lambda q: cols[block, q], block)
+
+    def near_tile(block, k, j):
+        total = dot(cols[end0, 0] if j == 0 else near[j - 1, 0], cols[block, 0])
+        for q in (1, 2, 3):
+            total += dot(cols[end0, q] if j == 0 else near[j - 1, q], cols[block, q])
+        tiles[k, j] = total
+        tile_copy(block, k, j).start()
+
+    def finish_fit():
+        for j in (2, 3):
+            fit_wait(2, j)
+            fit_copy(3, j ^ 1).start()
+        for j in (1, 2, 3):
+            fit_wait(1, j)
+            fit_wait(3, j)
+        multiply(
+            lambda q: a_ref[row_slice(f), :] if q == 0 else rows[q - 1, row_slice(f), :], r
+        )
+
+    fit_copy(2, 0).start()
+    fit_copy(1, 0).start()
+    send_own(0)
+    fit_copy(2, 1).start()
+    for j in (1, 2, 3):
+        fit_copy(1, j).start()
+    fit_wait(1, 0)
+    send_own(1)
+
+    @pl.when(is_inner)
+    def _():
+        pass_on(inner1, 0, FAR)
+        pass_on(end0, 0, FAR)
+        near_copy(1, 1).start()
+
+    fit_wait(2, 0)
+    send_own(2)
+    fit_copy(2, 2).start()
+    fit_wait(2, 1)
+    fit_copy(3, 0).start()
+    fit_copy(2, 3).start()
+    fit_copy(3, 1).start()
+    fit_wait(3, 0)
+    send_own(3)
+
+    @pl.when(is_inner)
+    def _():
+        near_copy(2, 2).start()
+        plane_wait(far_inner0, 0)
+        for q in (1, 2, 3):
+            pass_on(end0, q, FAR)
+            near_copy(1, q ^ 1).start()
+            near_copy(2, q ^ 2).start()
+            pass_on(far_inner0, q, MATE)
+        finish_fit()
+        pass_on(end1, 0, FAR)
+        for q in (1, 2, 3):
+            plane_wait(inner1, q)
+        multiply_block(inner1)
+        multiply_block(end0)
+        multiply_block(far_inner0)
+        near_copy(2, 2).wait_recv()
+        near_copy(3, 3).start()
+        plane_wait(far_end0, 0)
+        for q in quarters:
+            near_copy(1, q).wait_recv()
+        for j in (0, 1):
+            near_tile(far_inner0, 0, j)
+        pass_on(far_end0, 1, MATE)
+        plane_wait(far_inner1, 0)
+        for q in (1, 2, 3):
+            plane_wait(far_inner1, q)
+        for j in (0, 1):
+            near_tile(far_inner1, 1, j)
+        multiply_block(far_inner1)
+        for q in (3, 0, 1):
+            near_copy(2, q).wait_recv()
+            near_copy(3, q ^ 1).start()
+        for q in (2, 3):
+            pass_on(far_end0, q, MATE)
+        for j in (0, 1):
+            near_tile(far_end0, 2, j)
+        for q in quarters:
+            near_copy(3, q).wait_recv()
+        for j in (2, 3):
+            near_tile(far_inner0, 0, j)
+            near_tile(far_inner1, 1, j)
+            near_tile(far_end0, 2, j)
+        multiply_block(far_end0)
+        for q in (1, 2, 3):
+            plane_wait(end1, q)
+        multiply_block(end1)
+        for q in quarters:
+            plane_wait(far_end1, q)
+        for j in quarters:
+            near_tile(far_end1, 3, j)
+        multiply_block(far_end1)
+
+    @pl.when(is_end)
+    def _():
+        for q in quarters:
+            pass_on(end1, q, PARTNER)
+            pass_on(inner0, q, MATE)
+        finish_fit()
+        multiply_block(end1)
+        multiply_block(inner0)
+        for q in quarters:
+            plane_wait(inner1, q)
+        multiply_block(inner1)
+        for k, block in enumerate((far_inner0, far_inner1, far_end0, far_end1)):
+            for j in quarters:
+                tile_copy(block, k, j).wait_recv()
+            out_copy(block).start()
+
+    for q in quarters:
+        plane_copy(PARTNER, r, q).wait_send()
+        plane_copy(MATE, r, q).wait_send()
+        for j in (1, 2, 3):
+            fit_copy(j, q).wait_send()
+
+    @pl.when(is_inner)
+    def _():
+        for q in quarters:
+            plane_copy(FAR, r, q).wait_send()
+            plane_copy(FAR, end0, q).wait_send()
+            for j in (1, 2, 3):
+                near_copy(j, q).wait_send()
+            if q > 0:
+                plane_copy(MATE, far_inner0, q).wait_send()
+                plane_copy(MATE, far_end0, q).wait_send()
+        plane_copy(FAR, inner1, 0).wait_send()
+        plane_copy(FAR, end1, 0).wait_send()
+        for k, block in enumerate((far_inner0, far_inner1, far_end0, far_end1)):
+            for j in quarters:
+                tile_copy(block, k, j).wait_send()
+
+    @pl.when(is_end)
+    def _():
+        for q in quarters:
+            plane_copy(PARTNER, end1, q).wait_send()
+            plane_copy(MATE, inner0, q).wait_send()
+
+    for block in range(Y_SIZE * Z_SIZE):
+        out_copy(block).wait()
+
+
+def per_device(factors):
+    row_count, local_funcs, occupied = factors.shape
+    groups = lax.axis_size("fit")
+    blocks = lax.axis_size("row")
+    if (groups, blocks) != (4, Y_SIZE * Z_SIZE):
+        return gathered_by_collectives(factors)
+    sub = row_count // groups
+    width = local_funcs * occupied
+    out_shape = jax.ShapeDtypeStruct((row_count, blocks * sub), jnp.float32)
+    out = pl.pallas_call(
+        kernel,
+        out_shape=out_shape,
+        in_specs=[pl.BlockSpec(memory_space=pltpu.VMEM)],
+        out_specs=pl.BlockSpec(memory_space=pl.ANY),
+        scratch_shapes=[
+            pltpu.VMEM((row_count, blocks * sub), jnp.float32),
+            pltpu.VMEM((groups - 1, row_count, width), factors.dtype),
+            pltpu.VMEM((groups - 1, groups, sub, width), factors.dtype),
+            pltpu.VMEM((blocks, groups, sub, width), factors.dtype),
+            pltpu.VMEM((groups, groups, sub, sub), jnp.float32),
+            pltpu.SemaphoreType.DMA((3, 4)),
+            pltpu.SemaphoreType.DMA((3, 4)),
+            pltpu.SemaphoreType.DMA((3, 4)),
+            pltpu.SemaphoreType.DMA((3, 4)),
+            pltpu.SemaphoreType.DMA((3, blocks, 4)),
+            pltpu.SemaphoreType.DMA((blocks, 4)),
+            pltpu.SemaphoreType.DMA((4, 4)),
+            pltpu.SemaphoreType.DMA((4, 4)),
+            pltpu.SemaphoreType.DMA((blocks,)),
+        ],
+        compiler_params=pltpu.CompilerParams(
+            collective_id=0, has_side_effects=True, vmem_limit_bytes=62 * 2**20
+        ),
+        cost_estimate=pl.CostEstimate(
+            flops=2 * row_count * blocks * sub * groups * width,
+            bytes_accessed=4 * row_count * blocks * sub,
+            transcendentals=0,
+        ),
+    )(factors.reshape(row_count, width))
+    return out.reshape(1, row_count, blocks * sub)
+
+
 def solution(mesh):
     return jax.shard_map(
         per_device,

time: 662 us -> 246 us (0.37)
  waiting for transfers between devices: 517 us -> 0 us
  Pallas kernels: 0 us -> 232 us
  blocking collectives: 72.9 us -> 0 us
  matrix products: 34.4 us -> 0 us
  between operations: 13.4 us -> 0.02 us
  local copies, waits for them, and re-layouts: 24.2 us -> 14 us
    all_gather x2 -> x0, waiting for transfers between devices: 517 us -> none  [the longest x1 482 us: per_device(): columns = lax.all_gather(mine, 'row', axis=0)]
    pallas_call x0 -> x1, Pallas kernels: none -> 232 us  [per_device(): pl.pallas_call(kernel, out_shape=out_shape, in_specs=[pl.BlockSpec(memory...]
    all_to_all x1 -> x0, blocking collectives: 72.9 us -> none  [per_device(): mine = lax.all_to_all(pieces, 'fit', split_axis=0, concat_axis=0)]
    dot_general x1 -> x0, matrix products: 34.4 us -> none  [per_device(): lax.dot_general(rows, columns, (((0, 2), (1, 3)), ((), ())), preferred_el...]
    reshape x3 -> x1, local copies, waits for them, and re-layouts: 15.3 us -> 2.93 us  [per_device(): factors.reshape(row_count, width)]
    unnamed x1 -> x2, local copies, waits for them, and re-layouts: 3.18 us -> 11.1 us
  transfers between devices with their start and end apart: 2 -> 0, of which waited for: 2 -> 0; matrix products, arithmetic and copies ran while one was open for 1% -> 0% of each run, Pallas kernels for 0% -> 0%
where the time goes in v3:
time: 246 us
  Pallas kernels  232 us (94%)
  local copies, waits for them, and re-layouts  14 us (6%)
    pallas_call x1, Pallas kernels, per_device(): pl.pallas_call(kernel, out_shape=out_shape, in_specs=[pl.BlockSpec(memory...  232 us
    unnamed x2, local copies, waits for them, and re-layouts  11.1 us

profile of v3, /device:TPU:0, one launch (start us, length us, event | category | flops | bytes accessed | tf_op | source)
XLA Modules:
  0.0 246.1 jit_solution(10139957401296998223)
XLA Ops:
  0.0 3.2 %copy.3 = bf16[1024,3,512]{0,2,1:T(8,128)(2,1)S(1)} copy(bf16[1024,3,512]{2,0,1:T(8,128)(2,1)} %param.1) | data formatting | bytes 6291456 | tf_op args[0]
  3.2 2.9 %copy.4.a_ref = bf16[1024,1536]{1,0:T(8,128)(2,1)} copy(bf16[1024,1536]{0,1:T(8,128)(2,1)S(1)} %bitcast.2) | data formatting | bytes 6291456 | tf_op jit(solution)/shard_map/reshape | solution.py:360
  6.1 232.1 %shard_map.17 = f32[1024,2048]{1,0:T(8,128)} custom-call(bf16[1024,1536]{1,0:T(8,128)(2,1)} %copy.4.a_ref), custom_call_target="tpu_custom_call" | custom-call | flops 25769803776 | bytes 8388608 | tf_op jit(solution)/shard_map/pallas_call | solution.py:331
  238.2 7.9 %copy.6 = f32[1,1024,2048]{2,1,0:T(8,128)} copy(f32[1,1024,2048]{2,1,0:T(8,128)} %bitcast.3) | data formatting | bytes 16777216

commit v4 on v3

--- a/solution.py
+++ b/solution.py
@@ -25,8 +25,8 @@
     return out.reshape(1, row_count, blocks * sub_width)
 
 
-def kernel(a_ref, out_ref, acc, rows, near, cols, tiles, fit_send, fit_recv, near_send, near_recv,
-           send_sem, recv_sem, tile_send, tile_recv, out_sem):
+def kernel(a_hbm, out_ref, a_ref, acc, rows, near, cols, tiles, fit_send, fit_recv, near_send, near_recv,
+           send_sem, recv_sem, tile_send, tile_recv, out_sem, load_sem):
     f = lax.axis_index("fit")
     r = lax.axis_index("row")
     z = r // Y_SIZE
@@ -35,7 +35,7 @@
     x_peer = (f + 2) % 4
     diagonal = (core_mate + 2) % 4
     subs = (f, core_mate, x_peer, diagonal)
-    row_count, width = a_ref.shape
+    row_count, width = a_hbm.shape
     sub = row_count // 4
     half = z // 2
     end_z, inner_z = 3 * half, 1 + half
@@ -79,7 +79,7 @@
             target, s = x_peer, subs[2 ^ j]
         else:
             target, s = core_mate, subs[1 ^ j]
-        source = rows.at[1, row_slice(s)] if q == 3 else a_ref.at[row_slice(s)]
+        source = rows.at[1, row_slice(s)] if q == 3 else a_hbm.at[row_slice(s)]
         return pltpu.make_async_remote_copy(
             src_ref=source,
             dst_ref=rows.at[q - 1, row_slice(s)],
@@ -134,10 +134,10 @@
             plane_copy(direction, block, q).start()
 
     def send_own(q):
-        source = (a_ref if q == 0 else rows.at[q - 1]).at[row_slice(f)]
+        source = (a_hbm if q == 0 else rows.at[q - 1]).at[row_slice(f)]
         pl.when(is_inner)(lambda: plane_copy(FAR, r, q, source).start())
         plane_copy(PARTNER, r, q, source).start()
-        plane_copy(MATE, r, q, source).start()
+        pl.when(is_end | (q == 0))(lambda: plane_copy(MATE, r, q, source).start())
 
     def tile_copy(block, k, j):
         return pltpu.make_async_remote_copy(
@@ -182,13 +182,17 @@
         tiles[k, j] = total
         tile_copy(block, k, j).start()
 
+    load = pltpu.make_async_copy(a_hbm, a_ref, load_sem)
+
+    def spread_x_peer(j):
+        fit_wait(2, j)
+        fit_copy(3, j ^ 1).start()
+
     def finish_fit():
-        for j in (2, 3):
-            fit_wait(2, j)
-            fit_copy(3, j ^ 1).start()
         for j in (1, 2, 3):
             fit_wait(1, j)
             fit_wait(3, j)
+        load.wait()
         multiply(
             lambda q: a_ref[row_slice(f), :] if q == 0 else rows[q - 1, row_slice(f), :], r
         )
@@ -199,88 +203,96 @@
     fit_copy(2, 1).start()
     for j in (1, 2, 3):
         fit_copy(1, j).start()
+    load.start()
     fit_wait(1, 0)
     send_own(1)
 
     @pl.when(is_inner)
     def _():
-        pass_on(inner1, 0, FAR)
-        pass_on(end0, 0, FAR)
+        plane_wait(end0, 0)
         near_copy(1, 1).start()
 
     fit_wait(2, 0)
     send_own(2)
-    fit_copy(2, 2).start()
+    pl.when(is_end)(lambda: fit_copy(2, 2).start())
+    pl.when(is_inner)(lambda: near_copy(2, 2).start())
     fit_wait(2, 1)
     fit_copy(3, 0).start()
-    fit_copy(2, 3).start()
+    pl.when(is_end)(lambda: fit_copy(2, 3).start())
     fit_copy(3, 1).start()
     fit_wait(3, 0)
     send_own(3)
 
     @pl.when(is_inner)
     def _():
-        near_copy(2, 2).start()
-        plane_wait(far_inner0, 0)
+        pass_on(far_inner0, 0, MATE)
         for q in (1, 2, 3):
+            pass_on(far_inner0, q, MATE)
             pass_on(end0, q, FAR)
             near_copy(1, q ^ 1).start()
             near_copy(2, q ^ 2).start()
-            pass_on(far_inner0, q, MATE)
-        finish_fit()
+        plane_copy(FAR, end0, 0).start()
+        fit_copy(2, 2).start()
+        fit_copy(2, 3).start()
+        for q in (2, 3):
+            near_copy(2, q).wait_recv()
+            near_copy(3, q ^ 1).start()
         pass_on(end1, 0, FAR)
-        for q in (1, 2, 3):
-            plane_wait(inner1, q)
-        multiply_block(inner1)
-        multiply_block(end0)
-        multiply_block(far_inner0)
-        near_copy(2, 2).wait_recv()
-        near_copy(3, 3).start()
-        plane_wait(far_end0, 0)
+        pass_on(far_end0, 1, MATE)
+        near_copy(2, 0).wait_recv()
+        near_copy(3, 1).start()
         for q in quarters:
             near_copy(1, q).wait_recv()
+            plane_wait(far_inner1, q)
         for j in (0, 1):
             near_tile(far_inner0, 0, j)
-        pass_on(far_end0, 1, MATE)
-        plane_wait(far_inner1, 0)
-        for q in (1, 2, 3):
-            plane_wait(far_inner1, q)
-        for j in (0, 1):
             near_tile(far_inner1, 1, j)
-        multiply_block(far_inner1)
-        for q in (3, 0, 1):
-            near_copy(2, q).wait_recv()
-            near_copy(3, q ^ 1).start()
-        for q in (2, 3):
-            pass_on(far_end0, q, MATE)
-        for j in (0, 1):
-            near_tile(far_end0, 2, j)
+        near_copy(2, 1).wait_recv()
+        near_copy(3, 0).start()
+        pass_on(far_end0, 2, MATE)
         for q in quarters:
             near_copy(3, q).wait_recv()
         for j in (2, 3):
             near_tile(far_inner0, 0, j)
             near_tile(far_inner1, 1, j)
+        pass_on(far_end0, 3, MATE)
+        plane_copy(MATE, r, 1, rows.at[0, row_slice(f)]).start()
+        spread_x_peer(2)
+        plane_wait(far_end0, 0)
+        for j in quarters:
             near_tile(far_end0, 2, j)
+        spread_x_peer(3)
+        finish_fit()
+        multiply_block(end0)
+        multiply_block(far_inner0)
+        multiply_block(far_inner1)
+        for q in quarters:
+            plane_wait(far_end1, q)
+        for j in quarters:
+            near_tile(far_end1, 3, j)
         multiply_block(far_end0)
+        multiply_block(far_end1)
         for q in (1, 2, 3):
             plane_wait(end1, q)
         multiply_block(end1)
         for q in quarters:
-            plane_wait(far_end1, q)
-        for j in quarters:
-            near_tile(far_end1, 3, j)
-        multiply_block(far_end1)
+            plane_wait(inner1, q)
+        multiply_block(inner1)
 
     @pl.when(is_end)
     def _():
         for q in quarters:
             pass_on(end1, q, PARTNER)
             pass_on(inner0, q, MATE)
+        spread_x_peer(2)
+        spread_x_peer(3)
         finish_fit()
         multiply_block(end1)
         multiply_block(inner0)
-        for q in quarters:
-            plane_wait(inner1, q)
+        plane_wait(inner1, 0)
+        plane_wait(inner1, 1)
+        pass_on(inner1, 2, PARTNER)
+        pass_on(inner1, 3, PARTNER)
         multiply_block(inner1)
         for k, block in enumerate((far_inner0, far_inner1, far_end0, far_end1)):
             for j in quarters:
@@ -289,21 +301,21 @@
 
     for q in quarters:
         plane_copy(PARTNER, r, q).wait_send()
-        plane_copy(MATE, r, q).wait_send()
         for j in (1, 2, 3):
             fit_copy(j, q).wait_send()
+    for q in (0, 1):
+        plane_copy(MATE, r, q).wait_send()
 
     @pl.when(is_inner)
     def _():
         for q in quarters:
             plane_copy(FAR, r, q).wait_send()
             plane_copy(FAR, end0, q).wait_send()
+            plane_copy(MATE, far_inner0, q).wait_send()
             for j in (1, 2, 3):
                 near_copy(j, q).wait_send()
             if q > 0:
-                plane_copy(MATE, far_inner0, q).wait_send()
                 plane_copy(MATE, far_end0, q).wait_send()
-        plane_copy(FAR, inner1, 0).wait_send()
         plane_copy(FAR, end1, 0).wait_send()
         for k, block in enumerate((far_inner0, far_inner1, far_end0, far_end1)):
             for j in quarters:
@@ -314,6 +326,9 @@
         for q in quarters:
             plane_copy(PARTNER, end1, q).wait_send()
             plane_copy(MATE, inner0, q).wait_send()
+            if q > 1:
+                plane_copy(MATE, r, q).wait_send()
+                plane_copy(PARTNER, inner1, q).wait_send()
 
     for block in range(Y_SIZE * Z_SIZE):
         out_copy(block).wait()
@@ -331,9 +346,10 @@
     out = pl.pallas_call(
         kernel,
         out_shape=out_shape,
-        in_specs=[pl.BlockSpec(memory_space=pltpu.VMEM)],
+        in_specs=[pl.BlockSpec(memory_space=pl.ANY)],
         out_specs=pl.BlockSpec(memory_space=pl.ANY),
         scratch_shapes=[
+            pltpu.VMEM((row_count, width), factors.dtype),
             pltpu.VMEM((row_count, blocks * sub), jnp.float32),
             pltpu.VMEM((groups - 1, row_count, width), factors.dtype),
             pltpu.VMEM((groups - 1, groups, sub, width), factors.dtype),
@@ -348,6 +364,7 @@
             pltpu.SemaphoreType.DMA((4, 4)),
             pltpu.SemaphoreType.DMA((4, 4)),
             pltpu.SemaphoreType.DMA((blocks,)),
+            pltpu.SemaphoreType.DMA,
         ],
         compiler_params=pltpu.CompilerParams(
             collective_id=0, has_side_effects=True, vmem_limit_bytes=62 * 2**20

time: 246 us -> 220 us (0.89)
  Pallas kernels: 232 us -> 204 us
    pallas_call x1, Pallas kernels: 232 us -> 204 us  [per_device(): pl.pallas_call(kernel, out_shape=out_shape, in_specs=[pl.BlockSpec(memory...]
where the time goes in v4:
time: 220 us; the launch traced here: 218 us
  Pallas kernels  204 us (93%)
  local copies, waits for them, and re-layouts  14 us (6%)
    pallas_call x1, Pallas kernels, per_device(): pl.pallas_call(kernel, out_shape=out_shape, in_specs=[pl.BlockSpec(memory...  204 us
    unnamed x2, local copies, waits for them, and re-layouts  11.1 us

profile of v4, /device:TPU:0, one launch (start us, length us, event | category | flops | bytes accessed | tf_op | source)
XLA Modules:
  0.0 217.8 jit_solution(17804420255176857092)
XLA Ops:
  0.0 3.2 %copy.3 = bf16[1024,3,512]{0,2,1:T(8,128)(2,1)S(1)} copy(bf16[1024,3,512]{2,0,1:T(8,128)(2,1)} %param.1) | data formatting | bytes 6291456 | tf_op args[0]
  3.2 2.9 %copy.4.a_hbm = bf16[1024,1536]{1,0:T(8,128)(2,1)} copy(bf16[1024,1536]{0,1:T(8,128)(2,1)S(1)} %bitcast.2) | data formatting | bytes 6291456 | tf_op jit(solution)/shard_map/reshape | solution.py:377
  6.1 203.7 %shard_map.17 = f32[1024,2048]{1,0:T(8,128)} custom-call(bf16[1024,1536]{1,0:T(8,128)(2,1)} %copy.4.a_hbm), custom_call_target="tpu_custom_call" | custom-call | flops 25769803776 | bytes 8388608 | tf_op jit(solution)/shard_map/pallas_call | solution.py:346
  209.9 7.9 %copy.6 = f32[1,1024,2048]{2,1,0:T(8,128)} copy(f32[1,1024,2048]{2,1,0:T(8,128)} %bitcast.3) | data formatting | bytes 16777216

commit v5 on v4

--- a/solution.py
+++ b/solution.py
@@ -37,6 +37,7 @@
     subs = (f, core_mate, x_peer, diagonal)
     row_count, width = a_hbm.shape
     sub = row_count // 4
+    narrow = sub // 2
     half = z // 2
     end_z, inner_z = 3 * half, 1 + half
     far_inner_z, far_end_z = 2 - half, 3 - 3 * half
@@ -114,40 +115,64 @@
             device_id_type=MESH,
         )
 
-    def plane_copy(direction, block, q, source=None):
-        slot = cols.at[block, q]
+    def plane_copy(direction, block, q, h, source=None):
+        slot = cols.at[block, q, pl.ds(h * narrow, narrow)]
         return pltpu.make_async_remote_copy(
             src_ref=slot if source is None else source,
             dst_ref=slot,
-            send_sem=send_sem.at[direction, block, q],
-            recv_sem=recv_sem.at[block, q],
+            send_sem=send_sem.at[direction, block, 2 * q + h],
+            recv_sem=recv_sem.at[block, 2 * q + h],
             device_id=(f, targets[direction]),
             device_id_type=MESH,
         )
 
-    def plane_wait(block, q):
-        plane_copy(MATE, block, q).wait_recv()
-
-    def pass_on(block, q, *directions):
-        plane_wait(block, q)
-        for direction in directions:
-            plane_copy(direction, block, q).start()
+    def part_sent(direction, block, q):
+        for h in (0, 1):
+            plane_copy(direction, block, q, h).wait_send()
+
+    def plane_wait(block, q, halves=(0, 1)):
+        for h in halves:
+            plane_copy(MATE, block, q, h).wait_recv()
+
+    def pass_on(block, q, direction, halves=(0, 1)):
+        for h in halves:
+            plane_wait(block, q, (h,))
+            plane_copy(direction, block, q, h).start()
+
+    def send_own_half(direction, q, h):
+        here = pl.ds(pl.multiple_of(f * sub + h * narrow, narrow), narrow)
+        source = (a_hbm if q == 0 else rows.at[q - 1]).at[here]
+        plane_copy(direction, r, q, h, source).start()
 
     def send_own(q):
-        source = (a_hbm if q == 0 else rows.at[q - 1]).at[row_slice(f)]
-        pl.when(is_inner)(lambda: plane_copy(FAR, r, q, source).start())
-        plane_copy(PARTNER, r, q, source).start()
-        pl.when(is_end | (q == 0))(lambda: plane_copy(MATE, r, q, source).start())
-
-    def tile_copy(block, k, j):
+        for h in (0, 1):
+            pl.when(is_inner)(lambda: send_own_half(FAR, q, h))
+            send_own_half(PARTNER, q, h)
+            pl.when(is_end | (q == 0))(lambda: send_own_half(MATE, q, h))
+
+    def tile_copy(block, k, j, h, size):
         return pltpu.make_async_remote_copy(
-            src_ref=tiles.at[k, j],
-            dst_ref=acc.at[row_slice(subs[j]), col_slice(block)],
-            send_sem=tile_send.at[k, j],
-            recv_sem=tile_recv.at[k, j],
+            src_ref=tiles.at[k, j, :, pl.ds(h * narrow, size)],
+            dst_ref=acc.at[
+                row_slice(subs[j]),
+                pl.ds(pl.multiple_of(block * sub + h * narrow, narrow), size),
+            ],
+            send_sem=tile_send.at[k, 2 * j + h],
+            recv_sem=tile_recv.at[k, 2 * j + h],
             device_id=(f, partner),
             device_id_type=MESH,
         )
+
+    def tile_copies():
+        far = (far_inner0, far_inner1, far_end0, far_end1)
+        return [
+            [
+                tile_copy(block, k, j, h, sub if k < 2 else narrow)
+                for j in quarters
+                for h in ((0,) if k < 2 else (0, 1))
+            ]
+            for k, block in enumerate(far)
+        ]
 
     def out_copy(block):
         return pltpu.make_async_copy(
@@ -175,27 +200,38 @@
     def multiply_block(block):
         multiply(lambda q: cols[block, q], block)
 
-    def near_tile(block, k, j):
-        total = dot(cols[end0, 0] if j == 0 else near[j - 1, 0], cols[block, 0])
+    def multiply_rows(operand, block, early):
+        part = f // 2 if early else 1 - f // 2
+        here = pl.ds(pl.multiple_of(part * (2 * sub), 2 * sub), 2 * sub)
+        total = dot(a_ref[here, :], operand(0))
         for q in (1, 2, 3):
-            total += dot(cols[end0, q] if j == 0 else near[j - 1, q], cols[block, q])
-        tiles[k, j] = total
-        tile_copy(block, k, j).start()
+            total += dot(rows[q - 1, here, :], operand(q))
+        acc[here, col_slice(block)] = total
+        if not early:
+            out_copy(block).start()
+
+    def multiply_blocks(first, count, early):
+        @pl.loop(0, count)
+        def _(i):
+            block = first + i
+            multiply_rows(lambda q: cols[block, q], block, early)
+
+    def own_operand(q):
+        return a_ref[row_slice(f), :] if q == 0 else rows[q - 1, row_slice(f), :]
+
+    def near_tile(block, k, j, h, size):
+        here = pl.ds(h * narrow, size)
+        total = dot(cols[end0, 0] if j == 0 else near[j - 1, 0], cols[block, 0, here])
+        for q in (1, 2, 3):
+            total += dot(cols[end0, q] if j == 0 else near[j - 1, q], cols[block, q, here])
+        tiles[k, j, :, here] = total
+        tile_copy(block, k, j, h, size).start()
 
     load = pltpu.make_async_copy(a_hbm, a_ref, load_sem)
 
     def spread_x_peer(j):
         fit_wait(2, j)
         fit_copy(3, j ^ 1).start()
-
-    def finish_fit():
-        for j in (1, 2, 3):
-            fit_wait(1, j)
-            fit_wait(3, j)
-        load.wait()
-        multiply(
-            lambda q: a_ref[row_slice(f), :] if q == 0 else rows[q - 1, row_slice(f), :], r
-        )
 
     fit_copy(2, 0).start()
     fit_copy(1, 0).start()
@@ -225,54 +261,77 @@
 
     @pl.when(is_inner)
     def _():
+        plane_copy(FAR, end0, 0, 0).start()
         pass_on(far_inner0, 0, MATE)
         for q in (1, 2, 3):
             pass_on(far_inner0, q, MATE)
-            pass_on(end0, q, FAR)
+            plane_wait(end0, q)
+            plane_copy(FAR, end0, q, 0).start()
             near_copy(1, q ^ 1).start()
             near_copy(2, q ^ 2).start()
-        plane_copy(FAR, end0, 0).start()
+        for q in quarters:
+            plane_copy(FAR, end0, q, 1).start()
         fit_copy(2, 2).start()
         fit_copy(2, 3).start()
+        for q in quarters:
+            near_copy(1, q).wait_recv()
+        for j in (0, 1):
+            near_tile(far_inner0, 0, j, 0, sub)
         for q in (2, 3):
             near_copy(2, q).wait_recv()
             near_copy(3, q ^ 1).start()
-        pass_on(end1, 0, FAR)
-        pass_on(far_end0, 1, MATE)
+        pass_on(far_end0, 0, MATE, (0,))
+        load.wait()
+        fit_wait(1, 1)
+        fit_wait(3, 1)
+        multiply_rows(own_operand, r, True)
+        pass_on(far_end0, 1, MATE, (0,))
         near_copy(2, 0).wait_recv()
         near_copy(3, 1).start()
         for q in quarters:
-            near_copy(1, q).wait_recv()
             plane_wait(far_inner1, q)
         for j in (0, 1):
-            near_tile(far_inner0, 0, j)
-            near_tile(far_inner1, 1, j)
+            near_tile(far_inner1, 1, j, 0, sub)
+        pass_on(far_end0, 2, MATE, (0,))
         near_copy(2, 1).wait_recv()
         near_copy(3, 0).start()
-        pass_on(far_end0, 2, MATE)
+        pass_on(far_end0, 3, MATE, (0,))
         for q in quarters:
             near_copy(3, q).wait_recv()
         for j in (2, 3):
-            near_tile(far_inner0, 0, j)
-            near_tile(far_inner1, 1, j)
-        pass_on(far_end0, 3, MATE)
-        plane_copy(MATE, r, 1, rows.at[0, row_slice(f)]).start()
+            near_tile(far_inner0, 0, j, 0, sub)
+            near_tile(far_inner1, 1, j, 0, sub)
+        for j in quarters:
+            near_tile(far_end0, 2, j, 0, narrow)
+        pass_on(far_end0, 0, MATE, (1,))
+        for q in quarters:
+            plane_wait(far_end1, q, (0,))
+        for j in quarters:
+            near_tile(far_end1, 3, j, 0, narrow)
+        pass_on(far_end0, 1, MATE, (1,))
+        multiply_rows(lambda q: cols[end0, q], end0, True)
         spread_x_peer(2)
-        plane_wait(far_end0, 0)
+        pass_on(far_end0, 2, MATE, (1,))
+        multiply_blocks(node(far_inner_z, 0), 2, True)
+        pass_on(far_end0, 3, MATE, (1,))
+        for h in (0, 1):
+            send_own_half(MATE, 1, h)
         for j in quarters:
-            near_tile(far_end0, 2, j)
+            near_tile(far_end0, 2, j, 1, narrow)
         spread_x_peer(3)
-        finish_fit()
-        multiply_block(end0)
-        multiply_block(far_inner0)
-        multiply_block(far_inner1)
-        for q in quarters:
-            plane_wait(far_end1, q)
+        multiply_rows(lambda q: cols[far_end0, q], far_end0, True)
+        for q in quarters:
+            plane_wait(far_end1, q, (1,))
         for j in quarters:
-            near_tile(far_end1, 3, j)
-        multiply_block(far_end0)
-        multiply_block(far_end1)
-        for q in (1, 2, 3):
+            near_tile(far_end1, 3, j, 1, narrow)
+        multiply_rows(lambda q: cols[far_end1, q], far_end1, True)
+        for j in (2, 3):
+            fit_wait(1, j)
+            fit_wait(3, j)
+        multiply_rows(own_operand, r, False)
+        multiply_rows(lambda q: cols[end0, q], end0, False)
+        multiply_blocks(4 * (1 - half), 4, False)
+        for q in quarters:
             plane_wait(end1, q)
         multiply_block(end1)
         for q in quarters:
@@ -286,7 +345,11 @@
             pass_on(inner0, q, MATE)
         spread_x_peer(2)
         spread_x_peer(3)
-        finish_fit()
+        load.wait()
+        for j in (1, 2, 3):
+            fit_wait(1, j)
+            fit_wait(3, j)
+        multiply(own_operand, r)
         multiply_block(end1)
         multiply_block(inner0)
         plane_wait(inner1, 0)
@@ -294,41 +357,40 @@
         pass_on(inner1, 2, PARTNER)
         pass_on(inner1, 3, PARTNER)
         multiply_block(inner1)
-        for k, block in enumerate((far_inner0, far_inner1, far_end0, far_end1)):
-            for j in quarters:
-                tile_copy(block, k, j).wait_recv()
+        far = (far_inner0, far_inner1, far_end0, far_end1)
+        for block, copies in zip(far, tile_copies()):
+            for copy in copies:
+                copy.wait_recv()
             out_copy(block).start()
 
     for q in quarters:
-        plane_copy(PARTNER, r, q).wait_send()
+        part_sent(PARTNER, r, q)
         for j in (1, 2, 3):
             fit_copy(j, q).wait_send()
     for q in (0, 1):
-        plane_copy(MATE, r, q).wait_send()
+        part_sent(MATE, r, q)
 
     @pl.when(is_inner)
     def _():
         for q in quarters:
-            plane_copy(FAR, r, q).wait_send()
-            plane_copy(FAR, end0, q).wait_send()
-            plane_copy(MATE, far_inner0, q).wait_send()
+            part_sent(FAR, r, q)
+            part_sent(FAR, end0, q)
+            part_sent(MATE, far_inner0, q)
+            part_sent(MATE, far_end0, q)
             for j in (1, 2, 3):
                 near_copy(j, q).wait_send()
-            if q > 0:
-                plane_copy(MATE, far_end0, q).wait_send()
-        plane_copy(FAR, end1, 0).wait_send()
-        for k, block in enumerate((far_inner0, far_inner1, far_end0, far_end1)):
-            for j in quarters:
-                tile_copy(block, k, j).wait_send()
+        for copies in tile_copies():
+            for copy in copies:
+                copy.wait_send()
 
     @pl.when(is_end)
     def _():
         for q in quarters:
-            plane_copy(PARTNER, end1, q).wait_send()
-            plane_copy(MATE, inner0, q).wait_send()
+            part_sent(PARTNER, end1, q)
+            part_sent(MATE, inner0, q)
             if q > 1:
-                plane_copy(MATE, r, q).wait_send()
-                plane_copy(PARTNER, inner1, q).wait_send()
+                part_sent(MATE, r, q)
+                part_sent(PARTNER, inner1, q)
 
     for block in range(Y_SIZE * Z_SIZE):
         out_copy(block).wait()
@@ -359,10 +421,10 @@
             pltpu.SemaphoreType.DMA((3, 4)),
             pltpu.SemaphoreType.DMA((3, 4)),
             pltpu.SemaphoreType.DMA((3, 4)),
-            pltpu.SemaphoreType.DMA((3, blocks, 4)),
-            pltpu.SemaphoreType.DMA((blocks, 4)),
-            pltpu.SemaphoreType.DMA((4, 4)),
-            pltpu.SemaphoreType.DMA((4, 4)),
+            pltpu.SemaphoreType.DMA((3, blocks, 8)),
+            pltpu.SemaphoreType.DMA((blocks, 8)),
+            pltpu.SemaphoreType.DMA((4, 8)),
+            pltpu.SemaphoreType.DMA((4, 8)),
             pltpu.SemaphoreType.DMA((blocks,)),
             pltpu.SemaphoreType.DMA,
         ],

time: 220 us -> 226 us (1.027)
  the two profiles are of different devices: /device:TPU:0 before, /device:TPU:9 now
where the time goes in v5:
time: 226 us
  Pallas kernels  212 us (94%)
  local copies, waits for them, and re-layouts  14 us (6%)
    pallas_call x1, Pallas kernels, per_device(): pl.pallas_call(kernel, out_shape=out_shape, in_specs=[pl.BlockSpec(memory...  212 us
    unnamed x2, local copies, waits for them, and re-layouts  11.1 us

profile of v5, /device:TPU:9, one launch (start us, length us, event | category | flops | bytes accessed | tf_op | source)
XLA Modules:
  0.0 225.5 jit_solution(7531358040378477543)
XLA Ops:
  0.0 3.2 %copy.3 = bf16[1024,3,512]{0,2,1:T(8,128)(2,1)S(1)} copy(bf16[1024,3,512]{2,0,1:T(8,128)(2,1)} %param.1) | data formatting | bytes 6291456 | tf_op args[0]
  3.2 2.9 %copy.4.a_hbm = bf16[1024,1536]{1,0:T(8,128)(2,1)} copy(bf16[1024,1536]{0,1:T(8,128)(2,1)S(1)} %bitcast.2) | data formatting | bytes 6291456 | tf_op jit(solution)/shard_map/reshape | solution.py:439
  6.1 211.5 %shard_map.17 = f32[1024,2048]{1,0:T(8,128)} custom-call(bf16[1024,1536]{1,0:T(8,128)(2,1)} %copy.4.a_hbm), custom_call_target="tpu_custom_call" | custom-call | flops 25769803776 | bytes 8388608 | tf_op jit(solution)/shard_map/pallas_call | solution.py:408
  217.6 7.9 %copy.6 = f32[1,1024,2048]{2,1,0:T(8,128)} copy(f32[1,1024,2048]{2,1,0:T(8,128)} %bitcast.3) | data formatting | bytes 16777216
